TPU v7x, 256 devices: a whole 4x4x8 slice. The times are simulated.
256 devices in a mesh: uly: 4 (over x), inner: 16 (over y, z_lo), outer: 4 (over z_hi, core).
Axes of the slice: x: 4, y: 4, z: 8 (z_hi: 2, z_lo: 4; z = z_hi * 4 + z_lo), core: 2. Of those that a mesh axis runs over, the one named last changes fastest.
Arguments:
- query: bfloat16 [32768, 8192], P(('uly', 'inner', 'outer')), may hold values from -6 to 6
- key_proj: bfloat16 [32768, 512], P(('uly', 'inner', 'outer')), may hold values from -5 to 5
- value_projection: bfloat16 [32768, 512], P(('uly', 'inner', 'outer')), may hold values from -6 to 6
- upstream: bfloat16 [32768, 8192], P(('uly', 'inner', 'outer')), may hold values from -6 to 6
- doc_start: int32 [4, 8192], P(None, ('inner', 'outer')), may hold values from 0 to 32767
Outputs:
- attn_out: bfloat16 [32768, 8192], P(('uly', 'inner', 'outer'))
- grad_query: bfloat16 [32768, 8192], P(('uly', 'inner', 'outer'))
- grad_key: bfloat16 [32768, 512], P(('uly', 'inner', 'outer'))
- grad_value: bfloat16 [32768, 512], P(('uly', 'inner', 'outer'))
All inputs are finite; a program needn't handle non-finite values.
Results may differ from a plain program's by a relative error of at most 0.035.
Values may be sent and summed in bfloat16 or wider, within the bound.
A program may use at most 128 MiB of HBM per device.

v0:
```python
import functools
import math

import jax
import jax.numpy as jnp
from jax import lax
from jax.experimental import pallas as pl
from jax.experimental.pallas import tpu as pltpu
from jax.sharding import PartitionSpec as P

MESH = pl.DeviceIdType.MESH
D = 128
T = 128
HEADS = 4
R = HEADS * T
S = 3 * T
ROWS = 128
MASKED = -1e30

NN = (((1,), (0,)), ((), ()))


def dot(a, b):
    return lax.dot_general(a, b, NN, preferred_element_type=jnp.float32)


def kernel(
    mesh_shape, groups, heads,
    q_hbm, k_hbm, v_hbm, up_hbm, st_hbm,
    o_vm, gq_vm, gk_vm, gv_vm,
    q_vm, up_vm, st_vm, kv, fan_in, fan_out, tri, bias,
    s_0, s_1, w_0, w_1,
    acc, own, old, xsnd, xrcv, zsnd, zrcv,
    load_sem, st_sem, own_sem, prev_send, prev_recv, old_send, old_recv,
    gx_send, gx_recv, gz_send, gz_recv,
):
    n_inner, n_outer = mesh_shape
    blocks = n_inner * n_outer
    chunks = 4 * blocks
    width = heads * D
    per_group = heads // HEADS
    stages = groups * per_group
    steps = per_group // 2
    scale = D ** -0.5
    rate = scale * math.log2(math.e)

    u = lax.axis_index("uly")
    b = lax.axis_index("inner") * n_outer + lax.axis_index("outer")
    late = u // 2
    half = u - 2 * late
    span = b + late * (2 * blocks - 1 - 2 * b)
    chunk = 2 * span + half
    odd = half == 1

    def device_of(c):
        s = c // 2
        is_late = s // blocks
        blk = s + is_late * (2 * blocks - 1 - 2 * s)
        return (c - 2 * s + 2 * is_late, blk // n_outer, blk % n_outer)

    partner = (u + 1 - 2 * half, lax.axis_index("inner"), lax.axis_index("outer"))
    after = device_of((chunk + 2) % chunks)
    before = device_of((chunk + chunks - 2) % chunks)

    def cols(g):
        return pl.ds(pl.multiple_of(g * width, width), width)

    def load(g):
        return (
            pltpu.make_async_copy(q_hbm.at[:, cols(g)], q_vm.at[g], load_sem.at[g, 0]),
            pltpu.make_async_copy(up_hbm.at[:, cols(g)], up_vm.at[g], load_sem.at[g, 1]),
        )

    def load_own(g):
        return tuple(
            pltpu.make_async_copy(
                src.at[:, pl.ds(g * D, D)], kv.at[g, i, pl.ds(0, T)], own_sem.at[g, i])
            for i, src in enumerate((k_hbm, v_hbm))
        )

    def send_old(g):
        return pltpu.make_async_remote_copy(
            src_ref=kv.at[g, :, pl.ds(0, T)], dst_ref=kv.at[g, :, pl.ds(2 * T, T)],
            send_sem=old_send.at[g], recv_sem=old_recv.at[g],
            device_id=after, device_id_type=MESH)

    def send_prev(g):
        return pltpu.make_async_remote_copy(
            src_ref=kv.at[g, :, pl.ds(pl.multiple_of(half * (2 * T), T), T)],
            dst_ref=kv.at[g, :, pl.ds(T, T)],
            send_sem=prev_send.at[g], recv_sem=prev_recv.at[g],
            device_id=partner, device_id_type=MESH)

    def grad_x(g):
        return pltpu.make_async_remote_copy(
            src_ref=xsnd.at[g], dst_ref=xrcv.at[g], send_sem=gx_send.at[g],
            recv_sem=gx_recv.at[g], device_id=partner, device_id_type=MESH)

    def grad_z(g):
        return pltpu.make_async_remote_copy(
            src_ref=zsnd.at[g], dst_ref=zrcv.at[g], send_sem=gz_send.at[g],
            recv_sem=gz_recv.at[g], device_id=before, device_id_type=MESH)

    barrier = pltpu.get_barrier_semaphore()
    for peer in (partner, after, before):
        pl.semaphore_signal(barrier, inc=1, device_id=peer, device_id_type=MESH)

    starts = pltpu.make_async_copy(st_hbm, st_vm, st_sem)
    for g in range(groups):
        for copy in load_own(g):
            copy.start()
    starts.start()
    for g in range(groups):
        for copy in load(g):
            copy.start()

    for copy in load_own(0):
        copy.wait()
    pl.semaphore_wait(barrier, 3)
    send_old(0).start()

    @pl.when(jnp.logical_not(odd))
    def _():
        send_prev(0).start()

    for g in range(1, groups):
        for copy in load_own(g):
            copy.wait()

    starts.wait()
    first = st_vm[0:1, :]
    for i in range(1, 4):
        first = jnp.where(u == i, st_vm[i : i + 1, :], first)
    first = first - chunk * T
    key_at = lax.broadcasted_iota(jnp.int32, (T, T), 0)
    query_at = lax.broadcasted_iota(jnp.int32, (T, T), 1)
    seen = (
        (key_at <= query_at) & (key_at >= first),
        key_at - T >= first,
        (key_at > query_at) & (key_at - 2 * T >= first),
    )
    near = jnp.where(seen[0] | seen[2], 0.0, MASKED)
    bias[:, :T] = near.T
    bias[:, T:] = jnp.where(seen[1], 0.0, MASKED).T
    tri[...] = jnp.where(key_at >= query_at, 1.0, 0.0).astype(jnp.bfloat16)
    fan_in[...] = jnp.zeros_like(fan_in)
    fan_out[...] = jnp.zeros_like(fan_out)

    send_old(0).wait_send()
    send_old(1).start()

    @pl.when(jnp.logical_not(odd))
    def _():
        for g in range(1, groups):
            send_prev(g).start()

    def forward_old(g):
        send_old(g).wait_recv()
        send_prev(g).start()

    @pl.when(odd)
    def _():
        forward_old(0)

    def begin_group(g):
        @pl.when(jnp.logical_not(odd))
        def _():
            send_old(g).wait_recv()

        send_prev(g).wait_recv()
        for copy in load(g):
            copy.wait()
        fan_in[g, :D, :S] = kv[g, 0].T
        fan_in[g, D:, S:] = kv[g, 1].T
        fan_out[g, :S, :D] = kv[g, 1]
        fan_out[g, S:, D:] = kv[g, 0]

    def lanes_of(n):
        at = (n % per_group) * R
        return [pl.ds(pl.multiple_of(at + i * D, D), D) for i in range(HEADS)]

    def rows_of(ref, n):
        return jnp.concatenate([ref[n // per_group, :, c] for c in lanes_of(n)], axis=0)

    def scores(n, s_out):
        n = jnp.minimum(n, stages - 1)
        both = jnp.concatenate([rows_of(q_vm, n), rows_of(up_vm, n)], axis=1)
        s_out[...] = dot(both, fan_in[n // per_group])

    def soften(s_ref, w_out):
        for at in range(0, R, ROWS):
            rows = slice(at, at + ROWS)
            own_k, mid_k, old_k = [slice(i * T, (i + 1) * T) for i in range(3)]
            own_v, mid_v, old_v = [slice(i * T, (i + 1) * T) for i in range(3, 6)]
            here = slice(at % T, at % T + ROWS)
            key_at = lax.broadcasted_iota(jnp.int32, (ROWS, T), 1)
            query_at = lax.broadcasted_iota(jnp.int32, (ROWS, T), 0) + at % T
            lower = key_at <= query_at
            s_mix = jnp.where(lower, s_ref[rows, own_k], s_ref[rows, old_k]) + bias[here, :T]
            s_mid = s_ref[rows, mid_k] + bias[here, T:]
            top = jnp.max(jnp.maximum(s_mix, s_mid), axis=1, keepdims=True)
            e_mix = jnp.exp2((s_mix - top) * rate)
            e_mid = jnp.exp2((s_mid - top) * rate)
            inverse = 1.0 / jnp.sum(e_mix + e_mid, axis=1, keepdims=True)
            dp_mix = jnp.where(lower, s_ref[rows, own_v], s_ref[rows, old_v])
            dp_mid = s_ref[rows, mid_v]
            w_mix = e_mix * inverse
            w_mid = e_mid * inverse
            delta = jnp.sum(w_mix * dp_mix + w_mid * dp_mid, axis=1, keepdims=True)
            ds_mix = w_mix * (dp_mix - delta)
            ds_mid = w_mid * (dp_mid - delta)
            for mix, mid, base in ((w_mix, w_mid, 0), (ds_mix, ds_mid, S)):
                mix = mix.astype(jnp.bfloat16)
                own_part = mix * tri[here, :]
                w_out[rows, base : base + T] = own_part
                w_out[rows, base + T : base + 2 * T] = mid.astype(jnp.bfloat16)
                w_out[rows, base + 2 * T : base + S] = mix - own_part

    def results(n, w_ref):
        n = jnp.maximum(n, 0)
        both = dot(w_ref[...], fan_out[n // per_group])
        acc[1] += dot(rows_of(up_vm, n).T, w_ref[:, :S])
        acc[0] += dot(rows_of(q_vm, n).T, w_ref[:, S:])
        for i in range(HEADS):
            lanes = pl.ds(pl.multiple_of(n * R + i * D, D), D)
            rows = slice(i * T, (i + 1) * T)
            o_vm[:, lanes] = both[rows, :D].astype(jnp.bfloat16)
            gq_vm[:, lanes] = (both[rows, D:] * scale).astype(jnp.bfloat16)

    def finish_group(g):
        for i in range(2):
            grad = acc[i] * scale if i == 0 else acc[i]
            own[g, i] = grad[:, :T].T
            xsnd[g, i] = grad[:, T : 2 * T].T.astype(jnp.bfloat16)
            old[g, i] = grad[:, 2 * T :].T
        acc[...] = jnp.zeros_like(acc)
        grad_x(g).start()

        @pl.when(jnp.logical_not(odd))
        def _():
            zsnd[g] = old[g].astype(jnp.bfloat16)
            grad_z(g).start()

    def pass_back(g):
        @pl.when(odd)
        def _():
            grad_x(g).wait_recv()
            zsnd[g] = (old[g] + xrcv[g].astype(jnp.float32)).astype(jnp.bfloat16)
            grad_z(g).start()

    begin_group(0)
    acc[...] = jnp.zeros_like(acc)
    w_1[...] = jnp.zeros_like(w_1)
    scores(0, s_0)

    def step(t, carry):
        g = t // steps
        i = t % steps
        n = 2 * t

        @pl.when(jnp.logical_and(i == 0, g < groups - 2))
        def _():
            send_old(g + 2).start()

        @pl.when(jnp.logical_and(i == steps - 1, g > 0))
        def _():
            pass_back(g - 1)

        @pl.when(jnp.logical_and(jnp.logical_and(i == steps - 1, g < groups - 1), odd))
        def _():
            forward_old(g + 1)

        scores(n + 1, s_1)
        soften(s_0, w_0)
        results(n - 1, w_1)

        @pl.when(jnp.logical_and(i == 0, g > 0))
        def _():
            finish_group(g - 1)

        @pl.when(jnp.logical_and(i == steps - 1, g < groups - 1))
        def _():
            begin_group(g + 1)

        scores(n + 2, s_0)
        soften(s_1, w_1)
        results(n, w_0)
        return carry

    lax.fori_loop(0, groups * steps, step, 0)
    results(stages - 1, w_1)
    finish_group(groups - 1)
    pass_back(groups - 1)

    for g in range(groups):
        @pl.when(jnp.logical_not(odd))
        def _():
            grad_x(g).wait_recv()
            own[g] += xrcv[g].astype(jnp.float32)

        grad_z(g).wait_recv()
        for i, out in enumerate((gk_vm, gv_vm)):
            out[:, g * D : (g + 1) * D] = (
                own[g, i] + zrcv[g, i].astype(jnp.float32)).astype(jnp.bfloat16)
    for g in range(groups):
        if g:
            send_old(g).wait_send()
        for copy in (send_prev(g), grad_x(g), grad_z(g)):
            copy.wait_send()


def write_out(*refs):
    count = len(refs) // 2
    sems = refs[-1]
    copies = [pltpu.make_async_copy(refs[i], refs[count + i], sems.at[i]) for i in range(count)]
    for copy in copies:
        copy.start()
    for copy in copies:
        copy.wait()


def shards(mesh_shape, query, key_proj, value_projection, upstream, doc_start):
    groups = key_proj.shape[1] // D
    heads = query.shape[1] // D // groups
    bf16, f32 = jnp.bfloat16, jnp.float32
    dma = pltpu.SemaphoreType.DMA
    vm = pltpu.VMEM
    wide = (groups, T, heads * D)
    stage = (R, 2 * S)
    in_hbm = pl.BlockSpec(memory_space=pltpu.HBM)
    in_vmem = pl.BlockSpec(memory_space=pltpu.VMEM)
    shapes = (query.shape, query.shape, key_proj.shape, key_proj.shape)
    args = [
        pltpu.with_memory_space_constraint(x, pltpu.HBM)
        for x in (query, key_proj, value_projection, upstream, doc_start)
    ]
    held = pl.pallas_call(
        functools.partial(kernel, mesh_shape, groups, heads),
        out_shape=tuple(pltpu.VMEM(shape, bf16) for shape in shapes),
        in_specs=[in_hbm] * 5,
        out_specs=(in_vmem,) * 4,
        scratch_shapes=[
            vm(wide, bf16), vm(wide, bf16),
            vm(doc_start.shape, jnp.int32),
            vm((groups, 2, 3 * T, D), bf16),
            vm((groups, 2 * D, 2 * S), bf16), vm((groups, 2 * S, 2 * D), bf16),
            vm((T, T), bf16), vm((T, 2 * T), f32),
            vm(stage, f32), vm(stage, f32), vm(stage, bf16), vm(stage, bf16),
            vm((2, D, 3 * T), f32),
            vm((groups, 2, T, D), f32), vm((groups, 2, T, D), f32),
            vm((groups, 2, T, D), bf16), vm((groups, 2, T, D), bf16),
            vm((groups, 2, T, D), bf16), vm((groups, 2, T, D), bf16),
            dma((groups, 2)), dma, dma((groups, 2)),
            dma((groups,)), dma((groups,)), dma((groups,)), dma((groups,)),
            dma((groups,)), dma((groups,)), dma((groups,)), dma((groups,)),
        ],
        compiler_params=pltpu.CompilerParams(
            collective_id=0, has_side_effects=True, vmem_limit_bytes=40 * 1024 * 1024),
        cost_estimate=pl.CostEstimate(
            flops=12 * query.size * 3 * T, bytes_accessed=8 * query.size,
            transcendentals=query.size * 2),
    )(*args)
    held = [pltpu.with_memory_space_constraint(x, pltpu.VMEM) for x in held]
    return pl.pallas_call(
        write_out,
        out_shape=tuple(pltpu.HBM(shape, bf16) for shape in shapes),
        in_specs=[in_vmem] * 4,
        out_specs=(in_hbm,) * 4,
        scratch_shapes=[dma((4,))],
        compiler_params=pltpu.CompilerParams(vmem_limit_bytes=8 * 1024 * 1024),
    )(*held)


def solution(mesh):
    mesh_shape = (mesh.shape["inner"], mesh.shape["outer"])
    rows = P(("uly", "inner", "outer"), None)
    return jax.shard_map(
        functools.partial(shards, mesh_shape), mesh=mesh,
        in_specs=(rows, rows, rows, rows, P(None, ("inner", "outer"))),
        out_specs=(rows, rows, rows, rows), check_vma=False)
```

profile of v0, /device:TPU:27, one launch (start us, length us, event | category | flops | bytes accessed | tf_op | source)
XLA Modules:
  0.0 53.8 jit_solution(11227736148357731703)
XLA Ops:
  0.6 51.1 %shard_map.84 = (bf16[128,8192]{1,0:T(8,128)(2,1)S(1)}, bf16[128,8192]{1,0:T(8,128)(2,1)S(1)}, bf16[128,512]{1,0:T(8,128)(2,1)S(1)}, bf16[128,512]{1,0:T(8,128)(2,1)S(1)}) custom-call(bf16[128,8192]{1,0:T(8,128)(2,1)} %q_hbm.1, bf16[128,512]{1,0:T(8,128)(2,1)} %k_hbm.1, bf16[128,512]{1,0:T(8,128)(2,1)} %v_hbm.1, bf16[128,8192]{1,0:T(8,128)(2,1)} %up_hbm.1, ...), custom_call_target="tpu_custom_call" | custom-call | flops 4831838208 | bytes 8388608 | tf_op jit(solution)/shard_map/pallas_call | solution.py:337
  51.7 2.1 %shard_map.85 = (bf16[128,8192]{1,0:T(8,128)(2,1)}, bf16[128,8192]{1,0:T(8,128)(2,1)}, bf16[128,512]{1,0:T(8,128)(2,1)}, bf16[128,512]{1,0:T(8,128)(2,1)}) custom-call(bf16[128,8192]{1,0:T(8,128)(2,1)S(1)} %get-tuple-element.8.refs_0_, bf16[128,8192]{1,0:T(8,128)(2,1)S(1)} %get-tuple-element.9.refs_1_, bf16[128,512]{1,0:T(8,128)(2,1)S(1)} %get-tuple-element.10.refs_2_, ...), custom_call_target="tpu_custom_call" | custom-call | tf_op jit(solution)/shard_map/pallas_call | solution.py:364
where the time goes:
time: 53.9 us; the launch traced here: 53.8 us
  Pallas kernels  53.2 us (99%)
  between operations  0.64 us (1%)
    pallas_call x1, Pallas kernels, shards(): pl.pallas_call(functools.partial(kernel, mesh_shape, groups, heads), out_...  51.1 us
    pallas_call x1, Pallas kernels, shards(): pl.pallas_call(write_out, out_shape=tuple((pltpu.HBM(shape, bf16) for sha...  2.11 us

commit v1 on v0

--- a/solution.py
+++ b/solution.py
@@ -29,7 +29,7 @@
     q_hbm, k_hbm, v_hbm, up_hbm, st_hbm,
     o_vm, gq_vm, gk_vm, gv_vm,
     q_vm, up_vm, st_vm, kv, fan_in, fan_out, tri, bias,
-    s_0, s_1, w_0, w_1,
+    s_0, s_1, w_0, w_1, q_t, up_t,
     acc, own, old, xsnd, xrcv, zsnd, zrcv,
     load_sem, st_sem, own_sem, prev_send, prev_recv, old_send, old_recv,
     gx_send, gx_recv, gz_send, gz_recv,
@@ -146,6 +146,15 @@
     fan_in[...] = jnp.zeros_like(fan_in)
     fan_out[...] = jnp.zeros_like(fan_out)
 
+    def spread(g, lo, hi):
+        fan_in[g, :D, lo:hi] = kv[g, 0, lo:hi].T
+        fan_in[g, D:, S + lo : S + hi] = kv[g, 1, lo:hi].T
+        fan_out[g, lo:hi, :D] = kv[g, 1, lo:hi]
+        fan_out[g, S + lo : S + hi, D:] = kv[g, 0, lo:hi]
+
+    for g in range(groups):
+        spread(g, 0, T)
+
     send_old(0).wait_send()
     send_old(1).start()
 
@@ -154,6 +163,24 @@
         for g in range(1, groups):
             send_prev(g).start()
 
+    def lanes_of(n):
+        at = (n % per_group) * R
+        return [pl.ds(pl.multiple_of(at + i * D, D), D) for i in range(HEADS)]
+
+    def rows_of(ref, n):
+        return jnp.concatenate([ref[n // per_group, :, c] for c in lanes_of(n)], axis=0)
+
+    for g in range(groups):
+        for copy in load(g):
+            copy.wait()
+
+    def turn(n, carry):
+        q_t[n] = rows_of(q_vm, n).T
+        up_t[n] = rows_of(up_vm, n).T
+        return carry
+
+    lax.fori_loop(0, stages, turn, 0)
+
     def forward_old(g):
         send_old(g).wait_recv()
         send_prev(g).start()
@@ -168,26 +195,14 @@
             send_old(g).wait_recv()
 
         send_prev(g).wait_recv()
-        for copy in load(g):
-            copy.wait()
-        fan_in[g, :D, :S] = kv[g, 0].T
-        fan_in[g, D:, S:] = kv[g, 1].T
-        fan_out[g, :S, :D] = kv[g, 1]
-        fan_out[g, S:, D:] = kv[g, 0]
-
-    def lanes_of(n):
-        at = (n % per_group) * R
-        return [pl.ds(pl.multiple_of(at + i * D, D), D) for i in range(HEADS)]
-
-    def rows_of(ref, n):
-        return jnp.concatenate([ref[n // per_group, :, c] for c in lanes_of(n)], axis=0)
+        spread(g, T, S)
 
     def scores(n, s_out):
         n = jnp.minimum(n, stages - 1)
         both = jnp.concatenate([rows_of(q_vm, n), rows_of(up_vm, n)], axis=1)
         s_out[...] = dot(both, fan_in[n // per_group])
 
-    def soften(s_ref, w_out):
+    def soften(s_ref, w_out, t):
         for at in range(0, R, ROWS):
             rows = slice(at, at + ROWS)
             own_k, mid_k, old_k = [slice(i * T, (i + 1) * T) for i in range(3)]
@@ -212,15 +227,18 @@
             for mix, mid, base in ((w_mix, w_mid, 0), (ds_mix, ds_mid, S)):
                 mix = mix.astype(jnp.bfloat16)
                 own_part = mix * tri[here, :]
-                w_out[rows, base : base + T] = own_part
-                w_out[rows, base + T : base + 2 * T] = mid.astype(jnp.bfloat16)
-                w_out[rows, base + 2 * T : base + S] = mix - own_part
-
-    def results(n, w_ref):
+                w_out[t, rows, base : base + T] = own_part
+                w_out[t, rows, base + T : base + 2 * T] = mid.astype(jnp.bfloat16)
+                w_out[t, rows, base + 2 * T : base + S] = mix - own_part
+
+    def key_results(n, w_ref, t):
         n = jnp.maximum(n, 0)
-        both = dot(w_ref[...], fan_out[n // per_group])
-        acc[1] += dot(rows_of(up_vm, n).T, w_ref[:, :S])
-        acc[0] += dot(rows_of(q_vm, n).T, w_ref[:, S:])
+        t = jnp.maximum(t, 0)
+        acc[1] += dot(up_t[n], w_ref[t, :, :S])
+        acc[0] += dot(q_t[n], w_ref[t, :, S:])
+
+    def row_results(n, w_ref, t):
+        both = dot(w_ref[t], fan_out[n // per_group])
         for i in range(HEADS):
             lanes = pl.ds(pl.multiple_of(n * R + i * D, D), D)
             rows = slice(i * T, (i + 1) * T)
@@ -250,7 +268,7 @@
 
     begin_group(0)
     acc[...] = jnp.zeros_like(acc)
-    w_1[...] = jnp.zeros_like(w_1)
+    w_1[0] = jnp.zeros(w_1.shape[1:], w_1.dtype)
     scores(0, s_0)
 
     def step(t, carry):
@@ -271,8 +289,8 @@
             forward_old(g + 1)
 
         scores(n + 1, s_1)
-        soften(s_0, w_0)
-        results(n - 1, w_1)
+        soften(s_0, w_0, t)
+        key_results(n - 1, w_1, t - 1)
 
         @pl.when(jnp.logical_and(i == 0, g > 0))
         def _():
@@ -283,14 +301,25 @@
             begin_group(g + 1)
 
         scores(n + 2, s_0)
-        soften(s_1, w_1)
-        results(n, w_0)
+        soften(s_1, w_1, t)
+        key_results(n, w_0, t)
         return carry
 
     lax.fori_loop(0, groups * steps, step, 0)
-    results(stages - 1, w_1)
+    key_results(stages - 1, w_1, stages // 2 - 1)
     finish_group(groups - 1)
-    pass_back(groups - 1)
+
+    def rest(t, carry):
+        row_results(2 * t, w_0, t)
+        row_results(2 * t + 1, w_1, t)
+
+        @pl.when(t == 2)
+        def _():
+            pass_back(groups - 1)
+
+        return carry
+
+    lax.fori_loop(0, stages // 2, rest, 0)
 
     for g in range(groups):
         @pl.when(jnp.logical_not(odd))
@@ -327,6 +356,9 @@
     vm = pltpu.VMEM
     wide = (groups, T, heads * D)
     stage = (R, 2 * S)
+    stages = groups * heads // HEADS
+    half = (stages // 2,) + stage
+    turned = (stages, D, R)
     in_hbm = pl.BlockSpec(memory_space=pltpu.HBM)
     in_vmem = pl.BlockSpec(memory_space=pltpu.VMEM)
     shapes = (query.shape, query.shape, key_proj.shape, key_proj.shape)
@@ -345,7 +377,7 @@
             vm((groups, 2, 3 * T, D), bf16),
             vm((groups, 2 * D, 2 * S), bf16), vm((groups, 2 * S, 2 * D), bf16),
             vm((T, T), bf16), vm((T, 2 * T), f32),
-            vm(stage, f32), vm(stage, f32), vm(stage, bf16), vm(stage, bf16),
+            vm(stage, f32), vm(stage, f32), vm(half, bf16), vm(half, bf16), vm(turned, bf16), vm(turned, bf16),
             vm((2, D, 3 * T), f32),
             vm((groups, 2, T, D), f32), vm((groups, 2, T, D), f32),
             vm((groups, 2, T, D), bf16), vm((groups, 2, T, D), bf16),
@@ -355,7 +387,7 @@
             dma((groups,)), dma((groups,)), dma((groups,)), dma((groups,)),
         ],
         compiler_params=pltpu.CompilerParams(
-            collective_id=0, has_side_effects=True, vmem_limit_bytes=40 * 1024 * 1024),
+            collective_id=0, has_side_effects=True, vmem_limit_bytes=48 * 1024 * 1024),
         cost_estimate=pl.CostEstimate(
             flops=12 * query.size * 3 * T, bytes_accessed=8 * query.size,
             transcendentals=query.size * 2),

time: 53.9 us -> 52.1 us (0.967)
  Pallas kernels: 53.2 us -> 51.4 us
    pallas_call x1, Pallas kernels: 51.1 us -> 49.3 us  [shards(): pl.pallas_call(functools.partial(kernel, mesh_shape, groups, heads), out_...]
where the time goes in v1:
time: 52.1 us; the launch traced here: 52 us
  Pallas kernels  51.4 us (99%)
  between operations  0.64 us (1%)
    pallas_call x1, Pallas kernels, shards(): pl.pallas_call(functools.partial(kernel, mesh_shape, groups, heads), out_...  49.3 us
    pallas_call x1, Pallas kernels, shards(): pl.pallas_call(write_out, out_shape=tuple((pltpu.HBM(shape, bf16) for sha...  2.11 us

profile of v1, /device:TPU:27, one launch (start us, length us, event | category | flops | bytes accessed | tf_op | source)
XLA Modules:
  0.0 52.0 jit_solution(159493045278701262)
XLA Ops:
  0.6 49.3 %shard_map.84 = (bf16[128,8192]{1,0:T(8,128)(2,1)S(1)}, bf16[128,8192]{1,0:T(8,128)(2,1)S(1)}, bf16[128,512]{1,0:T(8,128)(2,1)S(1)}, bf16[128,512]{1,0:T(8,128)(2,1)S(1)}) custom-call(bf16[128,8192]{1,0:T(8,128)(2,1)} %q_hbm.1, bf16[128,512]{1,0:T(8,128)(2,1)} %k_hbm.1, bf16[128,512]{1,0:T(8,128)(2,1)} %v_hbm.1, bf16[128,8192]{1,0:T(8,128)(2,1)} %up_hbm.1, ...), custom_call_target="tpu_custom_call" | custom-call | flops 4831838208 | bytes 8388608 | tf_op jit(solution)/shard_map/pallas_call | solution.py:369
  49.9 2.1 %shard_map.85 = (bf16[128,8192]{1,0:T(8,128)(2,1)}, bf16[128,8192]{1,0:T(8,128)(2,1)}, bf16[128,512]{1,0:T(8,128)(2,1)}, bf16[128,512]{1,0:T(8,128)(2,1)}) custom-call(bf16[128,8192]{1,0:T(8,128)(2,1)S(1)} %get-tuple-element.8.refs_0_, bf16[128,8192]{1,0:T(8,128)(2,1)S(1)} %get-tuple-element.9.refs_1_, bf16[128,512]{1,0:T(8,128)(2,1)S(1)} %get-tuple-element.10.refs_2_, ...), custom_call_target="tpu_custom_call" | custom-call | tf_op jit(solution)/shard_map/pallas_call | solution.py:396

commit v2 on v1

--- a/solution.py
+++ b/solution.py
@@ -27,12 +27,12 @@
 def kernel(
     mesh_shape, groups, heads,
     q_hbm, k_hbm, v_hbm, up_hbm, st_hbm,
-    o_vm, gq_vm, gk_vm, gv_vm,
-    q_vm, up_vm, st_vm, kv, fan_in, fan_out, tri, bias,
+    o_out, gq_out, gk_out, gv_out,
+    q_vm, up_vm, o_vm, gq_vm, gk_vm, gv_vm, st_vm, kv, fan_in, fan_out, tri, bias,
     s_0, s_1, w_0, w_1, q_t, up_t,
     acc, own, old, xsnd, xrcv, zsnd, zrcv,
     load_sem, st_sem, own_sem, prev_send, prev_recv, old_send, old_recv,
-    gx_send, gx_recv, gz_send, gz_recv,
+    gx_send, gx_recv, gz_send, gz_recv, out_sem, gout_sem,
 ):
     n_inner, n_outer = mesh_shape
     blocks = n_inner * n_outer
@@ -69,6 +69,12 @@
         return (
             pltpu.make_async_copy(q_hbm.at[:, cols(g)], q_vm.at[g], load_sem.at[g, 0]),
             pltpu.make_async_copy(up_hbm.at[:, cols(g)], up_vm.at[g], load_sem.at[g, 1]),
+        )
+
+    def store(g):
+        return (
+            pltpu.make_async_copy(o_vm.at[g], o_out.at[:, cols(g)], out_sem.at[g, 0]),
+            pltpu.make_async_copy(gq_vm.at[g], gq_out.at[:, cols(g)], out_sem.at[g, 1]),
         )
 
     def load_own(g):
@@ -155,7 +161,6 @@
     for g in range(groups):
         spread(g, 0, T)
 
-    send_old(0).wait_send()
     send_old(1).start()
 
     @pl.when(jnp.logical_not(odd))
@@ -170,16 +175,17 @@
     def rows_of(ref, n):
         return jnp.concatenate([ref[n // per_group, :, c] for c in lanes_of(n)], axis=0)
 
-    for g in range(groups):
-        for copy in load(g):
-            copy.wait()
-
     def turn(n, carry):
         q_t[n] = rows_of(q_vm, n).T
         up_t[n] = rows_of(up_vm, n).T
         return carry
 
-    lax.fori_loop(0, stages, turn, 0)
+    for g in range(groups):
+        for copy in load(g):
+            copy.wait()
+        lax.fori_loop(g * per_group, (g + 1) * per_group, turn, 0)
+        if g + 2 < groups:
+            send_old(g + 2).start()
 
     def forward_old(g):
         send_old(g).wait_recv()
@@ -238,12 +244,12 @@
         acc[0] += dot(q_t[n], w_ref[t, :, S:])
 
     def row_results(n, w_ref, t):
-        both = dot(w_ref[t], fan_out[n // per_group])
-        for i in range(HEADS):
-            lanes = pl.ds(pl.multiple_of(n * R + i * D, D), D)
+        g = n // per_group
+        both = dot(w_ref[t], fan_out[g])
+        for i, lanes in enumerate(lanes_of(n)):
             rows = slice(i * T, (i + 1) * T)
-            o_vm[:, lanes] = both[rows, :D].astype(jnp.bfloat16)
-            gq_vm[:, lanes] = (both[rows, D:] * scale).astype(jnp.bfloat16)
+            o_vm[g, :, lanes] = both[rows, :D].astype(jnp.bfloat16)
+            gq_vm[g, :, lanes] = (both[rows, D:] * scale).astype(jnp.bfloat16)
 
     def finish_group(g):
         for i in range(2):
@@ -276,10 +282,6 @@
         i = t % steps
         n = 2 * t
 
-        @pl.when(jnp.logical_and(i == 0, g < groups - 2))
-        def _():
-            send_old(g + 2).start()
-
         @pl.when(jnp.logical_and(i == steps - 1, g > 0))
         def _():
             pass_back(g - 1)
@@ -313,6 +315,11 @@
         row_results(2 * t, w_0, t)
         row_results(2 * t + 1, w_1, t)
 
+        @pl.when(t % steps == steps - 1)
+        def _():
+            for copy in store(t // steps):
+                copy.start()
+
         @pl.when(t == 2)
         def _():
             pass_back(groups - 1)
@@ -331,10 +338,19 @@
         for i, out in enumerate((gk_vm, gv_vm)):
             out[:, g * D : (g + 1) * D] = (
                 own[g, i] + zrcv[g, i].astype(jnp.float32)).astype(jnp.bfloat16)
-    for g in range(groups):
-        if g:
-            send_old(g).wait_send()
-        for copy in (send_prev(g), grad_x(g), grad_z(g)):
+    outs = [
+        pltpu.make_async_copy(src, dst, gout_sem.at[i])
+        for i, (src, dst) in enumerate(((gk_vm, gk_out), (gv_vm, gv_out)))
+    ]
+    for copy in outs:
+        copy.start()
+    for g in range(groups):
+        for copy in store(g):
+            copy.wait()
+    for copy in outs:
+        copy.wait()
+    for g in range(groups):
+        for copy in (send_old(g), send_prev(g), grad_x(g), grad_z(g)):
             copy.wait_send()
 
 
@@ -360,7 +376,7 @@
     half = (stages // 2,) + stage
     turned = (stages, D, R)
     in_hbm = pl.BlockSpec(memory_space=pltpu.HBM)
-    in_vmem = pl.BlockSpec(memory_space=pltpu.VMEM)
+    anywhere = pl.BlockSpec(memory_space=pl.ANY)
     shapes = (query.shape, query.shape, key_proj.shape, key_proj.shape)
     args = [
         pltpu.with_memory_space_constraint(x, pltpu.HBM)
@@ -370,9 +386,10 @@
         functools.partial(kernel, mesh_shape, groups, heads),
         out_shape=tuple(pltpu.VMEM(shape, bf16) for shape in shapes),
         in_specs=[in_hbm] * 5,
-        out_specs=(in_vmem,) * 4,
+        out_specs=(anywhere,) * 4,
         scratch_shapes=[
-            vm(wide, bf16), vm(wide, bf16),
+            vm(wide, bf16), vm(wide, bf16), vm(wide, bf16), vm(wide, bf16),
+            vm(key_proj.shape, bf16), vm(key_proj.shape, bf16),
             vm(doc_start.shape, jnp.int32),
             vm((groups, 2, 3 * T, D), bf16),
             vm((groups, 2 * D, 2 * S), bf16), vm((groups, 2 * S, 2 * D), bf16),
@@ -385,6 +402,7 @@
             dma((groups, 2)), dma, dma((groups, 2)),
             dma((groups,)), dma((groups,)), dma((groups,)), dma((groups,)),
             dma((groups,)), dma((groups,)), dma((groups,)), dma((groups,)),
+            dma((groups, 2)), dma((2,)),
         ],
         compiler_params=pltpu.CompilerParams(
             collective_id=0, has_side_effects=True, vmem_limit_bytes=48 * 1024 * 1024),
@@ -396,7 +414,7 @@
     return pl.pallas_call(
         write_out,
         out_shape=tuple(pltpu.HBM(shape, bf16) for shape in shapes),
-        in_specs=[in_vmem] * 4,
+        in_specs=[anywhere] * 4,
         out_specs=(in_hbm,) * 4,
         scratch_shapes=[dma((4,))],
         compiler_params=pltpu.CompilerParams(vmem_limit_bytes=8 * 1024 * 1024),

time: 52.1 us -> 52.9 us (1.015)
  Pallas kernels: 51.4 us -> 52.2 us
    pallas_call x1, Pallas kernels: 49.3 us -> 50.1 us  [shards(): pl.pallas_call(functools.partial(kernel, mesh_shape, groups, heads), out_...]
where the time goes in v2:
time: 52.9 us
  Pallas kernels  52.2 us (99%)
  between operations  0.64 us (1%)
    pallas_call x1, Pallas kernels, shards(): pl.pallas_call(functools.partial(kernel, mesh_shape, groups, heads), out_...  50.1 us
    pallas_call x1, Pallas kernels, shards(): pl.pallas_call(write_out, out_shape=tuple((pltpu.HBM(shape, bf16) for sha...  2.11 us

profile of v2, /device:TPU:27, one launch (start us, length us, event | category | flops | bytes accessed | tf_op | source)
XLA Modules:
  0.0 52.9 jit_solution(17776726019856586522)
XLA Ops:
  0.6 50.1 %shard_map.84 = (bf16[128,8192]{1,0:T(8,128)(2,1)S(1)}, bf16[128,8192]{1,0:T(8,128)(2,1)S(1)}, bf16[128,512]{1,0:T(8,128)(2,1)S(1)}, bf16[128,512]{1,0:T(8,128)(2,1)S(1)}) custom-call(bf16[128,8192]{1,0:T(8,128)(2,1)} %q_hbm.1, bf16[128,512]{1,0:T(8,128)(2,1)} %k_hbm.1, bf16[128,512]{1,0:T(8,128)(2,1)} %v_hbm.1, bf16[128,8192]{1,0:T(8,128)(2,1)} %up_hbm.1, ...), custom_call_target="tpu_custom_call" | custom-call | flops 4831838208 | bytes 8388608 | tf_op jit(solution)/shard_map/pallas_call | solution.py:385
  50.7 2.1 %shard_map.85 = (bf16[128,8192]{1,0:T(8,128)(2,1)}, bf16[128,8192]{1,0:T(8,128)(2,1)}, bf16[128,512]{1,0:T(8,128)(2,1)}, bf16[128,512]{1,0:T(8,128)(2,1)}) custom-call(bf16[128,8192]{1,0:T(8,128)(2,1)S(1)} %get-tuple-element.8.refs_0_, bf16[128,8192]{1,0:T(8,128)(2,1)S(1)} %get-tuple-element.9.refs_1_, bf16[128,512]{1,0:T(8,128)(2,1)S(1)} %get-tuple-element.10.refs_2_, ...), custom_call_target="tpu_custom_call" | custom-call | tf_op jit(solution)/shard_map/pallas_call | solution.py:414

commit v3 on v1

v3 whole, which is shorter than its diff:
```python
import functools
import math

import jax
import jax.numpy as jnp
from jax import lax
from jax.experimental import pallas as pl
from jax.experimental.pallas import tpu as pltpu
from jax.sharding import PartitionSpec as P

MESH = pl.DeviceIdType.MESH
D = 128
T = 128
HEADS = 4
R = HEADS * T
S = 3 * T
ROWS = 128
MASKED = -1e30

NN = (((1,), (0,)), ((), ()))


def dot(a, b):
    return lax.dot_general(a, b, NN, preferred_element_type=jnp.float32)


class Place:
    def __init__(self, mesh_shape):
        n_inner, n_outer = mesh_shape
        blocks = n_inner * n_outer
        self.chunks = 4 * blocks
        self.u = u = lax.axis_index("uly")
        b = lax.axis_index("inner") * n_outer + lax.axis_index("outer")
        late = u // 2
        self.half = u - 2 * late
        span = b + late * (2 * blocks - 1 - 2 * b)
        self.chunk = 2 * span + self.half
        self.odd = self.half == 1

        def device_of(c):
            at = c // 2
            is_late = at // blocks
            blk = at + is_late * (2 * blocks - 1 - 2 * at)
            return (c - 2 * at + 2 * is_late, blk // n_outer, blk % n_outer)

        self.partner = (u + 1 - 2 * self.half, lax.axis_index("inner"), lax.axis_index("outer"))
        self.after = device_of((self.chunk + 2) % self.chunks)
        self.before = device_of((self.chunk + self.chunks - 2) % self.chunks)

    def greet(self):
        barrier = pltpu.get_barrier_semaphore()
        for peer in (self.partner, self.after, self.before):
            pl.semaphore_signal(barrier, inc=1, device_id=peer, device_id_type=MESH)

    def wait(self):
        pl.semaphore_wait(pltpu.get_barrier_semaphore(), 3)


def gather(
    mesh_shape, groups, heads, k_hbm, v_hbm, q_hbm, up_hbm, st_hbm,
    q_vm, up_vm, q_t, up_t, fan_in, fan_out, tri, bias,
    kv, st_vm, own_sem, load_sem, st_sem, prev_send, prev_recv, old_send, old_recv,
):
    at = Place(mesh_shape)
    width = heads * D
    per_group = heads // HEADS
    at.greet()
    own = [
        pltpu.make_async_copy(
            src.at[:, pl.ds(g * D, D)], kv.at[g, i, pl.ds(0, T)], own_sem.at[g, i])
        for g in range(groups) for i, src in enumerate((k_hbm, v_hbm))
    ]
    starts = pltpu.make_async_copy(st_hbm, st_vm, st_sem)
    loads = [
        [
            pltpu.make_async_copy(
                src.at[:, pl.ds(g * width, width)], dst.at[g], load_sem.at[g, i])
            for i, (src, dst) in enumerate(((q_hbm, q_vm), (up_hbm, up_vm)))
        ]
        for g in range(groups)
    ]
    for copy in own + [starts] + sum(loads, []):
        copy.start()

    def send_old(g):
        return pltpu.make_async_remote_copy(
            src_ref=kv.at[g, :, pl.ds(0, T)], dst_ref=kv.at[g, :, pl.ds(2 * T, T)],
            send_sem=old_send.at[g], recv_sem=old_recv.at[g],
            device_id=at.after, device_id_type=MESH)

    def send_prev(g):
        return pltpu.make_async_remote_copy(
            src_ref=kv.at[g, :, pl.ds(pl.multiple_of(at.half * (2 * T), T), T)],
            dst_ref=kv.at[g, :, pl.ds(T, T)],
            send_sem=prev_send.at[g], recv_sem=prev_recv.at[g],
            device_id=at.partner, device_id_type=MESH)

    for copy in own:
        copy.wait()
    at.wait()
    for g in range(groups):
        send_old(g).start()

    @pl.when(jnp.logical_not(at.odd))
    def _():
        for g in range(groups):
            send_prev(g).start()

    starts.wait()
    u, chunk = at.u, at.chunk
    first = st_vm[0:1, :]
    for i in range(1, 4):
        first = jnp.where(u == i, st_vm[i : i + 1, :], first)
    first = first - chunk * T
    key_at = lax.broadcasted_iota(jnp.int32, (T, T), 0)
    query_at = lax.broadcasted_iota(jnp.int32, (T, T), 1)
    seen = (
        (key_at <= query_at) & (key_at >= first),
        key_at - T >= first,
        (key_at > query_at) & (key_at - 2 * T >= first),
    )
    near = jnp.where(seen[0] | seen[2], 0.0, MASKED)
    bias[:, :T] = near.T
    bias[:, T:] = jnp.where(seen[1], 0.0, MASKED).T
    tri[...] = jnp.where(key_at >= query_at, 1.0, 0.0).astype(jnp.bfloat16)
    fan_in[...] = jnp.zeros_like(fan_in)
    fan_out[...] = jnp.zeros_like(fan_out)

    def spread(g, lo, hi):
        fan_in[g, :D, lo:hi] = kv[g, 0, lo:hi].T
        fan_in[g, D:, S + lo : S + hi] = kv[g, 1, lo:hi].T
        fan_out[g, lo:hi, :D] = kv[g, 1, lo:hi]
        fan_out[g, S + lo : S + hi, D:] = kv[g, 0, lo:hi]

    for g in range(groups):
        spread(g, 0, T)

    def lanes_of(n):
        at = (n % per_group) * R
        return [pl.ds(pl.multiple_of(at + i * D, D), D) for i in range(HEADS)]

    def rows_of(ref, n):
        return jnp.concatenate([ref[n // per_group, :, c] for c in lanes_of(n)], axis=0)

    def turn(n, carry):
        q_t[n] = rows_of(q_vm, n).T
        up_t[n] = rows_of(up_vm, n).T
        return carry

    for g in range(groups):
        for copy in loads[g]:
            copy.wait()
        lax.fori_loop(g * per_group, (g + 1) * per_group, turn, 0)

    @pl.when(at.odd)
    def _():
        for g in range(groups):
            send_old(g).wait_recv()
            send_prev(g).start()

    @pl.when(jnp.logical_not(at.odd))
    def _():
        for g in range(groups):
            send_old(g).wait_recv()

    for g in range(groups):
        spread(g, 2 * T, S)
    for g in range(groups):
        send_prev(g).wait_recv()
        spread(g, T, 2 * T)
    for g in range(groups):
        send_prev(g).wait_send()
        send_old(g).wait_send()


def attend(
    groups, heads, q_vm, up_vm, q_t, up_t, fan_in, tri, bias, w_0, w_1, grads, s_0, s_1, acc,
):
    per_group = heads // HEADS
    stages = groups * per_group
    steps = per_group // 2
    scale = D ** -0.5
    rate = scale * math.log2(math.e)

    def lanes_of(n):
        at = (n % per_group) * R
        return [pl.ds(pl.multiple_of(at + i * D, D), D) for i in range(HEADS)]

    def rows_of(ref, n):
        return jnp.concatenate([ref[n // per_group, :, c] for c in lanes_of(n)], axis=0)

    def scores(n, s_out):
        n = jnp.minimum(n, stages - 1)
        both = jnp.concatenate([rows_of(q_vm, n), rows_of(up_vm, n)], axis=1)
        s_out[...] = dot(both, fan_in[n // per_group])

    def soften(s_ref, w_out, t):
        for at in range(0, R, ROWS):
            rows = slice(at, at + ROWS)
            own_k, mid_k, old_k = [slice(i * T, (i + 1) * T) for i in range(3)]
            own_v, mid_v, old_v = [slice(i * T, (i + 1) * T) for i in range(3, 6)]
            here = slice(at % T, at % T + ROWS)
            key_at = lax.broadcasted_iota(jnp.int32, (ROWS, T), 1)
            query_at = lax.broadcasted_iota(jnp.int32, (ROWS, T), 0) + at % T
            lower = key_at <= query_at
            s_mix = jnp.where(lower, s_ref[rows, own_k], s_ref[rows, old_k]) + bias[here, :T]
            s_mid = s_ref[rows, mid_k] + bias[here, T:]
            top = jnp.max(jnp.maximum(s_mix, s_mid), axis=1, keepdims=True)
            e_mix = jnp.exp2((s_mix - top) * rate)
            e_mid = jnp.exp2((s_mid - top) * rate)
            inverse = 1.0 / jnp.sum(e_mix + e_mid, axis=1, keepdims=True)
            dp_mix = jnp.where(lower, s_ref[rows, own_v], s_ref[rows, old_v])
            dp_mid = s_ref[rows, mid_v]
            w_mix = e_mix * inverse
            w_mid = e_mid * inverse
            delta = jnp.sum(w_mix * dp_mix + w_mid * dp_mid, axis=1, keepdims=True)
            ds_mix = w_mix * (dp_mix - delta)
            ds_mid = w_mid * (dp_mid - delta)
            for mix, mid, base in ((w_mix, w_mid, 0), (ds_mix, ds_mid, S)):
                mix = mix.astype(jnp.bfloat16)
                own_part = mix * tri[here, :]
                w_out[t, rows, base : base + T] = own_part
                w_out[t, rows, base + T : base + 2 * T] = mid.astype(jnp.bfloat16)
                w_out[t, rows, base + 2 * T : base + S] = mix - own_part

    def key_results(n, w_ref, t):
        n = jnp.maximum(n, 0)
        t = jnp.maximum(t, 0)
        acc[1] += dot(up_t[n], w_ref[t, :, :S])
        acc[0] += dot(q_t[n], w_ref[t, :, S:])

    def finish_group(g):
        for i in range(2):
            grads[g, i] = (acc[i] * scale if i == 0 else acc[i]).T
        acc[...] = jnp.zeros_like(acc)

    acc[...] = jnp.zeros_like(acc)
    w_1[0] = jnp.zeros(w_1.shape[1:], w_1.dtype)
    scores(0, s_0)

    def step(t, carry):
        g = t // steps
        n = 2 * t

        scores(n + 1, s_1)
        soften(s_0, w_0, t)
        key_results(n - 1, w_1, t - 1)

        @pl.when(jnp.logical_and(t % steps == 0, g > 0))
        def _():
            finish_group(g - 1)

        scores(n + 2, s_0)
        soften(s_1, w_1, t)
        key_results(n, w_0, t)
        return carry

    lax.fori_loop(0, groups * steps, step, 0)
    key_results(stages - 1, w_1, stages // 2 - 1)
    finish_group(groups - 1)


def scatter(
    mesh_shape, groups, heads, grads, w_0, w_1, fan_out,
    o_vm, gq_vm, gk_vm, gv_vm, xsnd, xrcv, zsnd, zrcv, gx_send, gx_recv, gz_send, gz_recv,
):
    at = Place(mesh_shape)
    per_group = heads // HEADS
    stages = groups * per_group
    scale = D ** -0.5
    at.greet()

    def grad_x(g):
        return pltpu.make_async_remote_copy(
            src_ref=xsnd.at[g], dst_ref=xrcv.at[g], send_sem=gx_send.at[g],
            recv_sem=gx_recv.at[g], device_id=at.partner, device_id_type=MESH)

    def grad_z(g):
        return pltpu.make_async_remote_copy(
            src_ref=zsnd.at[g], dst_ref=zrcv.at[g], send_sem=gz_send.at[g],
            recv_sem=gz_recv.at[g], device_id=at.before, device_id_type=MESH)

    for g in range(groups):
        for i in range(2):
            xsnd[g, i] = grads[g, i, T : 2 * T].astype(jnp.bfloat16)
    at.wait()
    for g in range(groups):
        grad_x(g).start()

    @pl.when(jnp.logical_not(at.odd))
    def _():
        for g in range(groups):
            for i in range(2):
                zsnd[g, i] = grads[g, i, 2 * T :].astype(jnp.bfloat16)
            grad_z(g).start()

    def pass_back(g):
        grad_x(g).wait_recv()
        for i in range(2):
            zsnd[g, i] = (
                grads[g, i, 2 * T :] + xrcv[g, i].astype(jnp.float32)).astype(jnp.bfloat16)
        grad_z(g).start()

    def row_results(n, w_ref, t):
        both = dot(w_ref[t], fan_out[n // per_group])
        for i in range(HEADS):
            lanes = pl.ds(pl.multiple_of(n * R + i * D, D), D)
            rows = slice(i * T, (i + 1) * T)
            o_vm[:, lanes] = both[rows, :D].astype(jnp.bfloat16)
            gq_vm[:, lanes] = (both[rows, D:] * scale).astype(jnp.bfloat16)

    def rest(t, carry):
        row_results(2 * t, w_0, t)
        row_results(2 * t + 1, w_1, t)

        @pl.when(jnp.logical_and(at.odd, jnp.logical_and(t >= 2, t < 2 + groups)))
        def _():
            pass_back(t - 2)

        return carry

    lax.fori_loop(0, stages // 2, rest, 0)

    @pl.when(jnp.logical_not(at.odd))
    def _():
        for g in range(groups):
            grad_x(g).wait_recv()

    for g in range(groups):
        grad_z(g).wait_recv()
        for i, out in enumerate((gk_vm, gv_vm)):
            mine = grads[g, i, :T] + zrcv[g, i].astype(jnp.float32)
            more = jnp.where(at.odd, 0.0, xrcv[g, i].astype(jnp.float32))
            out[:, g * D : (g + 1) * D] = (mine + more).astype(jnp.bfloat16)
    for g in range(groups):
        grad_x(g).wait_send()
        grad_z(g).wait_send()


def write_out(*refs):
    count = len(refs) // 2
    sems = refs[-1]
    copies = [pltpu.make_async_copy(refs[i], refs[count + i], sems.at[i]) for i in range(count)]
    for copy in copies:
        copy.start()
    for copy in copies:
        copy.wait()


def shards(mesh_shape, query, key_proj, value_projection, upstream, doc_start):
    groups = key_proj.shape[1] // D
    heads = query.shape[1] // D // groups
    stages = groups * heads // HEADS
    bf16, f32 = jnp.bfloat16, jnp.float32
    dma = pltpu.SemaphoreType.DMA
    vm = pltpu.VMEM
    in_hbm = pl.BlockSpec(memory_space=pltpu.HBM)
    in_vmem = pl.BlockSpec(memory_space=pltpu.VMEM)
    mib = 1024 * 1024
    shapes = (query.shape, query.shape, key_proj.shape, key_proj.shape)
    wide = vm((groups, T, heads * D), bf16)
    turned = vm((stages, D, R), bf16)
    weights = vm((stages // 2, R, 2 * S), bf16)
    block = vm((groups, 2, T, D), bf16)

    def held(*arrays):
        return [pltpu.with_memory_space_constraint(x, pltpu.VMEM) for x in arrays]

    q, up, q_t, up_t, fan_in, fan_out, tri, bias = pl.pallas_call(
        functools.partial(gather, mesh_shape, groups, heads),
        out_shape=(
            wide, wide, turned, turned,
            vm((groups, 2 * D, 2 * S), bf16), vm((groups, 2 * S, 2 * D), bf16),
            vm((T, T), bf16), vm((T, 2 * T), f32)),
        in_specs=[in_hbm] * 5,
        out_specs=(in_vmem,) * 8,
        scratch_shapes=[
            vm((groups, 2, S, D), bf16), vm(doc_start.shape, jnp.int32),
            dma((groups, 2)), dma((groups, 2)), dma] + [dma((groups,))] * 4,
        compiler_params=pltpu.CompilerParams(
            collective_id=0, has_side_effects=True, vmem_limit_bytes=8 * mib),
    )(*[
        pltpu.with_memory_space_constraint(x, pltpu.HBM)
        for x in (key_proj, value_projection, query, upstream, doc_start)
    ])
    w_0, w_1, grads = pl.pallas_call(
        functools.partial(attend, groups, heads),
        out_shape=(weights, weights, vm((groups, 2, S, D), f32)),
        in_specs=[in_vmem] * 7,
        out_specs=(in_vmem,) * 3,
        scratch_shapes=[vm((R, 2 * S), f32), vm((R, 2 * S), f32), vm((2, D, S), f32)],
        compiler_params=pltpu.CompilerParams(vmem_limit_bytes=16 * mib),
        cost_estimate=pl.CostEstimate(
            flops=8 * query.size * S, bytes_accessed=8 * query.size,
            transcendentals=query.size * 2),
    )(*held(q, up, q_t, up_t, fan_in, tri, bias))
    results = pl.pallas_call(
        functools.partial(scatter, mesh_shape, groups, heads),
        out_shape=tuple(vm(shape, bf16) for shape in shapes),
        in_specs=[in_vmem] * 4,
        out_specs=(in_vmem,) * 4,
        scratch_shapes=[block] * 4 + [dma((groups,))] * 4,
        compiler_params=pltpu.CompilerParams(
            collective_id=1, has_side_effects=True, vmem_limit_bytes=12 * mib),
    )(*held(grads, w_0, w_1, fan_out))
    return pl.pallas_call(
        write_out,
        out_shape=tuple(pltpu.HBM(shape, bf16) for shape in shapes),
        in_specs=[in_vmem] * 4,
        out_specs=(in_hbm,) * 4,
        scratch_shapes=[dma((4,))],
        compiler_params=pltpu.CompilerParams(vmem_limit_bytes=8 * mib),
    )(*held(*results))


def solution(mesh):
    mesh_shape = (mesh.shape["inner"], mesh.shape["outer"])
    rows = P(("uly", "inner", "outer"), None)
    return jax.shard_map(
        functools.partial(shards, mesh_shape), mesh=mesh,
        in_specs=(rows, rows, rows, rows, P(None, ("inner", "outer"))),
        out_specs=(rows, rows, rows, rows), check_vma=False)
```

time: 52.1 us -> 49.8 us (0.956)
  Pallas kernels: 51.4 us -> 49.1 us
    pallas_call x1 -> x3, Pallas kernels: 49.3 us -> 46.9 us  [the longest x1 19.2 us: shards(): pl.pallas_call(functools.partial(scatter, mesh_shape, groups, heads), out...]
where the time goes in v3:
time: 49.8 us; the launch traced here: 49.7 us
  Pallas kernels  49.1 us (99%)
  between operations  0.65 us (1%)
    pallas_call x1, Pallas kernels, shards(): pl.pallas_call(functools.partial(scatter, mesh_shape, groups, heads), out...  19.2 us
    pallas_call x1, Pallas kernels, shards(): pl.pallas_call(functools.partial(gather, mesh_shape, groups, heads), out_...  16.5 us
    pallas_call x1, Pallas kernels, shards(): pl.pallas_call(functools.partial(attend, groups, heads), out_shape=(weigh...  11.3 us
    pallas_call x1, Pallas kernels, shards(): pl.pallas_call(write_out, out_shape=tuple((pltpu.HBM(shape, bf16) for sha...  2.11 us

profile of v3, /device:TPU:27, one launch (start us, length us, event | category | flops | bytes accessed | tf_op | source)
XLA Modules:
  0.0 49.7 jit_solution(11727737200279665881)
XLA Ops:
  0.6 16.5 %shard_map.84 = (bf16[4,128,2048]{2,1,0:T(8,128)(2,1)S(1)}, bf16[4,128,2048]{2,1,0:T(8,128)(2,1)S(1)}, bf16[16,128,512]{2,1,0:T(8,128)(2,1)S(1)}, bf16[16,128,51...) custom-call(bf16[128,512]{1,0:T(8,128)(2,1)} %k_hbm.1, ...), custom_call_target="tpu_custom_call" | custom-call | tf_op jit(solution)/shard_map/pallas_call | solution.py:369
  17.1 11.3 %shard_map.85 = (bf16[8,512,768]{2,1,0:T(8,128)(2,1)S(1)}, bf16[8,512,768]{2,1,0:T(8,128)(2,1)S(1)}, f32[4,2,384,128]{3,2,1,0:T(8,128)S(1)}) custom-call(bf16[4,128,2048]{2,1,0:T(8,128)(2,1)S(1)} %get-tuple-element.19.q_vm, bf16[4,128,2048]{2,1,0:T(8,128)(2,1)S(1)} %get-tuple-element.20.up_vm, bf16[16,128,512]{2,1,0:T(8,128)(2,1)S(1)} %get-tuple-element.21.q_t, ...), custom_call_target="tpu_custom_call" | custom-call | flops 3221225472 | bytes 8388608 | tf_op jit(solution)/shard_map/pallas_call | solution.py:386
  28.4 19.2 %shard_map.86 = (bf16[128,8192]{1,0:T(8,128)(2,1)S(1)}, bf16[128,8192]{1,0:T(8,128)(2,1)S(1)}, bf16[128,512]{1,0:T(8,128)(2,1)S(1)}, bf16[128,512]{1,0:T(8,128)(2,1)S(1)}) custom-call(f32[4,2,384,128]{3,2,1,0:T(8,128)S(1)} %get-tuple-element.26.grads, bf16[8,512,768]{2,1,0:T(8,128)(2,1)S(1)} %get-tuple-element.27.w_0, ...), custom_call_target="tpu_custom_call" | custom-call | tf_op jit(solution)/shard_map/pallas_call | solution.py:397
  47.6 2.1 %shard_map.87 = (bf16[128,8192]{1,0:T(8,128)(2,1)}, bf16[128,8192]{1,0:T(8,128)(2,1)}, bf16[128,512]{1,0:T(8,128)(2,1)}, bf16[128,512]{1,0:T(8,128)(2,1)}) custom-call(bf16[128,8192]{1,0:T(8,128)(2,1)S(1)} %get-tuple-element.30.refs_0_, bf16[128,8192]{1,0:T(8,128)(2,1)S(1)} %get-tuple-element.31.refs_1_, bf16[128,512]{1,0:T(8,128)(2,1)S(1)} %get-tuple-element.32.refs_2_, ...), custom_call_target="tpu_custom_call" | custom-call | tf_op jit(solution)/shard_map/pallas_call | solution.py:406

commit v4 on v3

--- a/solution.py
+++ b/solution.py
@@ -174,13 +174,29 @@
 
 
 def attend(
-    groups, heads, q_vm, up_vm, q_t, up_t, fan_in, tri, bias, w_0, w_1, grads, s_0, s_1, acc,
+    mesh_shape, groups, heads,
+    q_vm, up_vm, q_t, up_t, fan_in, fan_out, tri, bias,
+    o_vm, gq_vm, gk_vm, gv_vm,
+    s_0, s_1, w_0, w_1, acc, own, old, xsnd, xrcv, zsnd, zrcv,
+    gx_send, gx_recv, gz_send, gz_recv,
 ):
+    at = Place(mesh_shape)
     per_group = heads // HEADS
     stages = groups * per_group
     steps = per_group // 2
     scale = D ** -0.5
     rate = scale * math.log2(math.e)
+    at.greet()
+
+    def grad_x(g):
+        return pltpu.make_async_remote_copy(
+            src_ref=xsnd.at[g], dst_ref=xrcv.at[g], send_sem=gx_send.at[g],
+            recv_sem=gx_recv.at[g], device_id=at.partner, device_id_type=MESH)
+
+    def grad_z(g):
+        return pltpu.make_async_remote_copy(
+            src_ref=zsnd.at[g], dst_ref=zrcv.at[g], send_sem=gz_send.at[g],
+            recv_sem=gz_recv.at[g], device_id=at.before, device_id_type=MESH)
 
     def lanes_of(n):
         at = (n % per_group) * R
@@ -229,78 +245,6 @@
         acc[1] += dot(up_t[n], w_ref[t, :, :S])
         acc[0] += dot(q_t[n], w_ref[t, :, S:])
 
-    def finish_group(g):
-        for i in range(2):
-            grads[g, i] = (acc[i] * scale if i == 0 else acc[i]).T
-        acc[...] = jnp.zeros_like(acc)
-
-    acc[...] = jnp.zeros_like(acc)
-    w_1[0] = jnp.zeros(w_1.shape[1:], w_1.dtype)
-    scores(0, s_0)
-
-    def step(t, carry):
-        g = t // steps
-        n = 2 * t
-
-        scores(n + 1, s_1)
-        soften(s_0, w_0, t)
-        key_results(n - 1, w_1, t - 1)
-
-        @pl.when(jnp.logical_and(t % steps == 0, g > 0))
-        def _():
-            finish_group(g - 1)
-
-        scores(n + 2, s_0)
-        soften(s_1, w_1, t)
-        key_results(n, w_0, t)
-        return carry
-
-    lax.fori_loop(0, groups * steps, step, 0)
-    key_results(stages - 1, w_1, stages // 2 - 1)
-    finish_group(groups - 1)
-
-
-def scatter(
-    mesh_shape, groups, heads, grads, w_0, w_1, fan_out,
-    o_vm, gq_vm, gk_vm, gv_vm, xsnd, xrcv, zsnd, zrcv, gx_send, gx_recv, gz_send, gz_recv,
-):
-    at = Place(mesh_shape)
-    per_group = heads // HEADS
-    stages = groups * per_group
-    scale = D ** -0.5
-    at.greet()
-
-    def grad_x(g):
-        return pltpu.make_async_remote_copy(
-            src_ref=xsnd.at[g], dst_ref=xrcv.at[g], send_sem=gx_send.at[g],
-            recv_sem=gx_recv.at[g], device_id=at.partner, device_id_type=MESH)
-
-    def grad_z(g):
-        return pltpu.make_async_remote_copy(
-            src_ref=zsnd.at[g], dst_ref=zrcv.at[g], send_sem=gz_send.at[g],
-            recv_sem=gz_recv.at[g], device_id=at.before, device_id_type=MESH)
-
-    for g in range(groups):
-        for i in range(2):
-            xsnd[g, i] = grads[g, i, T : 2 * T].astype(jnp.bfloat16)
-    at.wait()
-    for g in range(groups):
-        grad_x(g).start()
-
-    @pl.when(jnp.logical_not(at.odd))
-    def _():
-        for g in range(groups):
-            for i in range(2):
-                zsnd[g, i] = grads[g, i, 2 * T :].astype(jnp.bfloat16)
-            grad_z(g).start()
-
-    def pass_back(g):
-        grad_x(g).wait_recv()
-        for i in range(2):
-            zsnd[g, i] = (
-                grads[g, i, 2 * T :] + xrcv[g, i].astype(jnp.float32)).astype(jnp.bfloat16)
-        grad_z(g).start()
-
     def row_results(n, w_ref, t):
         both = dot(w_ref[t], fan_out[n // per_group])
         for i in range(HEADS):
@@ -309,32 +253,86 @@
             o_vm[:, lanes] = both[rows, :D].astype(jnp.bfloat16)
             gq_vm[:, lanes] = (both[rows, D:] * scale).astype(jnp.bfloat16)
 
+    def finish_group(g):
+        for i in range(2):
+            grad = acc[i] * scale if i == 0 else acc[i]
+            own[g, i] = grad[:, :T].T
+            xsnd[g, i] = grad[:, T : 2 * T].T.astype(jnp.bfloat16)
+            old[g, i] = grad[:, 2 * T :].T
+        acc[...] = jnp.zeros_like(acc)
+        grad_x(g).start()
+
+        @pl.when(jnp.logical_not(at.odd))
+        def _():
+            zsnd[g] = old[g].astype(jnp.bfloat16)
+            grad_z(g).start()
+
+    def pass_back(g):
+        @pl.when(at.odd)
+        def _():
+            grad_x(g).wait_recv()
+            zsnd[g] = (old[g] + xrcv[g].astype(jnp.float32)).astype(jnp.bfloat16)
+            grad_z(g).start()
+
+    acc[...] = jnp.zeros_like(acc)
+    w_1[0] = jnp.zeros(w_1.shape[1:], w_1.dtype)
+    scores(0, s_0)
+
+    def step(t, carry):
+        g = t // steps
+        i = t % steps
+        n = 2 * t
+
+        @pl.when(t == steps)
+        def _():
+            at.wait()
+
+        @pl.when(jnp.logical_and(i == steps - 1, g > 0))
+        def _():
+            pass_back(g - 1)
+
+        scores(n + 1, s_1)
+        soften(s_0, w_0, t)
+        key_results(n - 1, w_1, t - 1)
+
+        @pl.when(jnp.logical_and(i == 0, g > 0))
+        def _():
+            finish_group(g - 1)
+
+        scores(n + 2, s_0)
+        soften(s_1, w_1, t)
+        key_results(n, w_0, t)
+        return carry
+
+    lax.fori_loop(0, groups * steps, step, 0)
+    key_results(stages - 1, w_1, stages // 2 - 1)
+    finish_group(groups - 1)
+
     def rest(t, carry):
         row_results(2 * t, w_0, t)
         row_results(2 * t + 1, w_1, t)
 
-        @pl.when(jnp.logical_and(at.odd, jnp.logical_and(t >= 2, t < 2 + groups)))
-        def _():
-            pass_back(t - 2)
+        @pl.when(t == 2)
+        def _():
+            pass_back(groups - 1)
 
         return carry
 
     lax.fori_loop(0, stages // 2, rest, 0)
 
-    @pl.when(jnp.logical_not(at.odd))
-    def _():
-        for g in range(groups):
+    for g in range(groups):
+        @pl.when(jnp.logical_not(at.odd))
+        def _():
             grad_x(g).wait_recv()
-
-    for g in range(groups):
+            own[g] += xrcv[g].astype(jnp.float32)
+
         grad_z(g).wait_recv()
         for i, out in enumerate((gk_vm, gv_vm)):
-            mine = grads[g, i, :T] + zrcv[g, i].astype(jnp.float32)
-            more = jnp.where(at.odd, 0.0, xrcv[g, i].astype(jnp.float32))
-            out[:, g * D : (g + 1) * D] = (mine + more).astype(jnp.bfloat16)
-    for g in range(groups):
-        grad_x(g).wait_send()
-        grad_z(g).wait_send()
+            out[:, g * D : (g + 1) * D] = (
+                own[g, i] + zrcv[g, i].astype(jnp.float32)).astype(jnp.bfloat16)
+    for g in range(groups):
+        for copy in (grad_x(g), grad_z(g)):
+            copy.wait_send()
 
 
 def write_out(*refs):
@@ -383,26 +381,21 @@
         pltpu.with_memory_space_constraint(x, pltpu.HBM)
         for x in (key_proj, value_projection, query, upstream, doc_start)
     ])
-    w_0, w_1, grads = pl.pallas_call(
-        functools.partial(attend, groups, heads),
-        out_shape=(weights, weights, vm((groups, 2, S, D), f32)),
-        in_specs=[in_vmem] * 7,
-        out_specs=(in_vmem,) * 3,
-        scratch_shapes=[vm((R, 2 * S), f32), vm((R, 2 * S), f32), vm((2, D, S), f32)],
-        compiler_params=pltpu.CompilerParams(vmem_limit_bytes=16 * mib),
+    results = pl.pallas_call(
+        functools.partial(attend, mesh_shape, groups, heads),
+        out_shape=tuple(vm(shape, bf16) for shape in shapes),
+        in_specs=[in_vmem] * 8,
+        out_specs=(in_vmem,) * 4,
+        scratch_shapes=[
+            vm((R, 2 * S), f32), vm((R, 2 * S), f32), weights, weights, vm((2, D, S), f32),
+            vm((groups, 2, T, D), f32), vm((groups, 2, T, D), f32),
+            block, block, block, block] + [dma((groups,))] * 4,
+        compiler_params=pltpu.CompilerParams(
+            collective_id=1, has_side_effects=True, vmem_limit_bytes=28 * mib),
         cost_estimate=pl.CostEstimate(
-            flops=8 * query.size * S, bytes_accessed=8 * query.size,
+            flops=12 * query.size * S, bytes_accessed=8 * query.size,
             transcendentals=query.size * 2),
-    )(*held(q, up, q_t, up_t, fan_in, tri, bias))
-    results = pl.pallas_call(
-        functools.partial(scatter, mesh_shape, groups, heads),
-        out_shape=tuple(vm(shape, bf16) for shape in shapes),
-        in_specs=[in_vmem] * 4,
-        out_specs=(in_vmem,) * 4,
-        scratch_shapes=[block] * 4 + [dma((groups,))] * 4,
-        compiler_params=pltpu.CompilerParams(
-            collective_id=1, has_side_effects=True, vmem_limit_bytes=12 * mib),
-    )(*held(grads, w_0, w_1, fan_out))
+    )(*held(q, up, q_t, up_t, fan_in, fan_out, tri, bias))
     return pl.pallas_call(
         write_out,
         out_shape=tuple(pltpu.HBM(shape, bf16) for shape in shapes),

time: 49.8 us -> 44.7 us (0.90)
  the two profiles are of different devices: /device:TPU:27 before, /device:TPU:51 now
where the time goes in v4:
time: 44.7 us; the launch traced here: 44.6 us
  Pallas kernels  44 us (98%)
  between operations  0.65 us (1%)
    pallas_call x1, Pallas kernels, shards(): pl.pallas_call(functools.partial(attend, mesh_shape, groups, heads), out_...  28 us
    pallas_call x1, Pallas kernels, shards(): pl.pallas_call(functools.partial(gather, mesh_shape, groups, heads), out_...  13.8 us
    pallas_call x1, Pallas kernels, shards(): pl.pallas_call(write_out, out_shape=tuple((pltpu.HBM(shape, bf16) for sha...  2.11 us

profile of v4, /device:TPU:51, one launch (start us, length us, event | category | flops | bytes accessed | tf_op | source)
XLA Modules:
  0.0 44.6 jit_solution(18227873744201157483)
XLA Ops:
  0.6 13.8 %shard_map.84 = (bf16[4,128,2048]{2,1,0:T(8,128)(2,1)S(1)}, bf16[4,128,2048]{2,1,0:T(8,128)(2,1)S(1)}, bf16[16,128,512]{2,1,0:T(8,128)(2,1)S(1)}, bf16[16,128,51...) custom-call(bf16[128,512]{1,0:T(8,128)(2,1)} %k_hbm.1, ...), custom_call_target="tpu_custom_call" | custom-call | tf_op jit(solution)/shard_map/pallas_call | solution.py:367
  14.5 28.0 %shard_map.85 = (bf16[128,8192]{1,0:T(8,128)(2,1)S(1)}, bf16[128,8192]{1,0:T(8,128)(2,1)S(1)}, bf16[128,512]{1,0:T(8,128)(2,1)S(1)}, bf16[128,512]{1,0:T(8,128)(2,1)S(1)}) custom-call(bf16[4,128,2048]{2,1,0:T(8,128)(2,1)S(1)} %get-tuple-element.16.q_vm, bf16[4,128,2048]{2,1,0:T(8,128)(2,1)S(1)} %get-tuple-element.17.up_vm, ...), custom_call_target="tpu_custom_call" | custom-call | flops 4831838208 | bytes 8388608 | tf_op jit(solution)/shard_map/pallas_call | solution.py:384
  42.5 2.1 %shard_map.86 = (bf16[128,8192]{1,0:T(8,128)(2,1)}, bf16[128,8192]{1,0:T(8,128)(2,1)}, bf16[128,512]{1,0:T(8,128)(2,1)}, bf16[128,512]{1,0:T(8,128)(2,1)}) custom-call(bf16[128,8192]{1,0:T(8,128)(2,1)S(1)} %get-tuple-element.24.refs_0_, bf16[128,8192]{1,0:T(8,128)(2,1)S(1)} %get-tuple-element.25.refs_1_, bf16[128,512]{1,0:T(8,128)(2,1)S(1)} %get-tuple-element.26.refs_2_, ...), custom_call_target="tpu_custom_call" | custom-call | tf_op jit(solution)/shard_map/pallas_call | solution.py:399

commit v5 on v4

--- a/solution.py
+++ b/solution.py
@@ -287,10 +287,6 @@
         def _():
             at.wait()
 
-        @pl.when(jnp.logical_and(i == steps - 1, g > 0))
-        def _():
-            pass_back(g - 1)
-
         scores(n + 1, s_1)
         soften(s_0, w_0, t)
         key_results(n - 1, w_1, t - 1)
@@ -302,6 +298,11 @@
         scores(n + 2, s_0)
         soften(s_1, w_1, t)
         key_results(n, w_0, t)
+
+        @pl.when(jnp.logical_and(i == steps - 1, g > 0))
+        def _():
+            pass_back(g - 1)
+
         return carry
 
     lax.fori_loop(0, groups * steps, step, 0)

time: 44.7 us -> 43.5 us (0.973)
  Pallas kernels: 44 us -> 42.7 us
    pallas_call x1, Pallas kernels: 28 us -> 26.8 us  [shards(): pl.pallas_call(functools.partial(attend, mesh_shape, groups, heads), out_...]
where the time goes in v5:
time: 43.5 us; the launch traced here: 43.4 us
  Pallas kernels  42.7 us (98%)
  between operations  0.65 us (1%)
    pallas_call x1, Pallas kernels, shards(): pl.pallas_call(functools.partial(attend, mesh_shape, groups, heads), out_...  26.8 us
    pallas_call x1, Pallas kernels, shards(): pl.pallas_call(functools.partial(gather, mesh_shape, groups, heads), out_...  13.8 us
    pallas_call x1, Pallas kernels, shards(): pl.pallas_call(write_out, out_shape=tuple((pltpu.HBM(shape, bf16) for sha...  2.11 us

profile of v5, /device:TPU:51, one launch (start us, length us, event | category | flops | bytes accessed | tf_op | source)
XLA Modules:
  0.0 43.4 jit_solution(1682100981774855277)
XLA Ops:
  0.6 13.8 %shard_map.84 = (bf16[4,128,2048]{2,1,0:T(8,128)(2,1)S(1)}, bf16[4,128,2048]{2,1,0:T(8,128)(2,1)S(1)}, bf16[16,128,512]{2,1,0:T(8,128)(2,1)S(1)}, bf16[16,128,51...) custom-call(bf16[128,512]{1,0:T(8,128)(2,1)} %k_hbm.1, ...), custom_call_target="tpu_custom_call" | custom-call | tf_op jit(solution)/shard_map/pallas_call | solution.py:368
  14.5 26.8 %shard_map.85 = (bf16[128,8192]{1,0:T(8,128)(2,1)S(1)}, bf16[128,8192]{1,0:T(8,128)(2,1)S(1)}, bf16[128,512]{1,0:T(8,128)(2,1)S(1)}, bf16[128,512]{1,0:T(8,128)(2,1)S(1)}) custom-call(bf16[4,128,2048]{2,1,0:T(8,128)(2,1)S(1)} %get-tuple-element.16.q_vm, bf16[4,128,2048]{2,1,0:T(8,128)(2,1)S(1)} %get-tuple-element.17.up_vm, ...), custom_call_target="tpu_custom_call" | custom-call | flops 4831838208 | bytes 8388608 | tf_op jit(solution)/shard_map/pallas_call | solution.py:385
  41.3 2.1 %shard_map.86 = (bf16[128,8192]{1,0:T(8,128)(2,1)}, bf16[128,8192]{1,0:T(8,128)(2,1)}, bf16[128,512]{1,0:T(8,128)(2,1)}, bf16[128,512]{1,0:T(8,128)(2,1)}) custom-call(bf16[128,8192]{1,0:T(8,128)(2,1)S(1)} %get-tuple-element.24.refs_0_, bf16[128,8192]{1,0:T(8,128)(2,1)S(1)} %get-tuple-element.25.refs_1_, bf16[128,512]{1,0:T(8,128)(2,1)S(1)} %get-tuple-element.26.refs_2_, ...), custom_call_target="tpu_custom_call" | custom-call | tf_op jit(solution)/shard_map/pallas_call | solution.py:400
